TPU v7x, 32 devices: a whole 2x2x4 slice. The times are simulated.
32 devices in a mesh: parts: 2 (over x), seq: 16 (over z, y, core).
Axes of the slice: x: 2, y: 2, z: 4, core: 2. Of those that a mesh axis runs over, the one named last changes fastest.
Arguments:
- frames: bfloat16 [8, 1024, 1024], P('parts', 'seq'), parts along dimension 0, may hold values from -10 to 10
- conv_weight: bfloat16 [128, 64, 1024], P('seq'), may hold values from -0.0625 to 0.0625
- conv_bias: float32 [1024], replicated, may hold values from -1 to 1
- w_qkv: bfloat16 [1024, 3, 16, 64], replicated, may hold values from -1 to 1
- w_out: bfloat16 [16, 64, 1024], replicated, may hold values from -1.5 to 1.5
Outputs:
- targets: bfloat16 [8, 1024, 1024], P('parts', 'seq'), parts along dimension 0
There are 2 independent parts, one for each index of `parts`. A program takes and returns all parts, laid end to end along the dimension named above; an argument that names none is the same for every part. Nothing has to cross between parts.
All inputs are finite; a program needn't handle non-finite values.
Results may differ from a plain program's by a relative error of at most 0.012.
The roundings to bfloat16 on the way count: a program that leaves them out, or rounds other values in their place, can miss the bound.
Values may be sent and summed in bfloat16 or wider, within the bound.
A program may use at most 192 MiB of HBM per device.

v0:
```python
import functools
import math

import jax
import jax.numpy as jnp
from jax import lax
from jax.experimental import pallas as pl
from jax.experimental.pallas import tpu as pltpu
from jax.sharding import PartitionSpec as P

GROUPS = 16
KERNEL = 128
MESH = pl.DeviceIdType.MESH
F32 = jnp.float32
BF16 = jnp.bfloat16


def mm(a, b):
    return jnp.dot(a, b, preferred_element_type=F32)


def pair(a, b):
    w = a.shape[-1] // 2
    return (
        jnp.concatenate([a[:, :w], b[:, :w]], axis=1),
        jnp.concatenate([a[:, w:], b[:, w:]], axis=1),
    )


def fused_kernel(
    n, rec, groups, taps, head,
    x_ref, w_ref, bias_ref, wq_ref, wo_ref, out_ref,
    sx, rx, rf, xs, sw, ew, k2, mf, m4, gg, lhs, qkv, ct, cx, res,
    sx_send, sx_recv, sw_send, sw_recv, z_send, y_send, c_send, g_recv,
    r_send, r_recv, t_send, t_recv,
):
    me = lax.axis_index("seq")
    width = x_ref.shape[2]
    frames = x_ref.shape[1]
    gw = width // groups
    pack = 256 // gw
    vs = frames // pack
    rows = rec * vs
    per = n // rec
    wide = width // per
    tap_pairs = w_ref.shape[0] // 2
    own_rec = me // per
    own_h = me % per

    barrier = pltpu.get_barrier_semaphore()

    def greet(k, carry):
        pl.semaphore_signal(barrier, inc=1, device_id={"seq": (me + k) % n}, device_id_type=MESH)
        return carry

    lax.fori_loop(1, n, greet, 0)

    count = rec * frames
    ri = lax.broadcasted_iota(jnp.int32, (count, count), 0)
    ci = lax.broadcasted_iota(jnp.int32, (count, count), 1)
    a_i, rest = ri // rows, ri % rows
    r_i, v_i = rest // vs, rest % vs
    perm = jnp.where(ci == r_i * frames + v_i * pack + a_i, 1.0, 0.0).astype(BF16)
    x2 = x_ref[...].reshape(count, width)
    for gp in range(groups // 2):
        moved = mm(perm, x2[:, gp * 128:(gp + 1) * 128]).astype(BF16)
        for ah in range(pack // 2):
            lo, hi = pair(
                moved[2 * ah * rows:(2 * ah + 1) * rows],
                moved[(2 * ah + 1) * rows:(2 * ah + 2) * rows],
            )
            sx[2 * gp, :, ah * 128:(ah + 1) * 128] = lo
            sx[2 * gp + 1, :, ah * 128:(ah + 1) * 128] = hi

    pl.semaphore_wait(barrier, n - 1)

    def x_copy(peer, slot):
        return pltpu.make_async_remote_copy(
            src_ref=sx.at[peer], dst_ref=rx.at[slot],
            send_sem=sx_send.at[peer], recv_sem=sx_recv.at[slot],
            device_id={"seq": peer}, device_id_type=MESH,
        )

    def w_copy(peer, slot):
        return pltpu.make_async_remote_copy(
            src_ref=sw.at[peer], dst_ref=ew.at[pl.ds(1 + slot * tap_pairs, tap_pairs)],
            send_sem=sw_send.at[peer], recv_sem=sw_recv.at[slot],
            device_id={"seq": peer}, device_id_type=MESH,
        )

    def start_x(k, carry):
        x_copy((me + k) % n, me).start()
        return carry

    lax.fori_loop(1, n, start_x, 0)
    for p in range(tap_pairs):
        for gp in range(groups // 2):
            lo, hi = pair(
                w_ref[2 * p, :, gp * 128:(gp + 1) * 128],
                w_ref[2 * p + 1, :, gp * 128:(gp + 1) * 128],
            )
            sw[2 * gp, p] = lo
            sw[2 * gp + 1, p] = hi

    def start_w(k, carry):
        w_copy((me + k) % n, me).start()
        return carry

    lax.fori_loop(1, n, start_w, 0)

    rx[me] = sx[me]
    ew[pl.ds(1 + me * tap_pairs, tap_pairs)] = sw[me]
    ew[0] = jnp.zeros_like(ew[0])
    ew[taps // 2 + 1] = jnp.zeros_like(ew[0])
    zero = jnp.zeros((rows, 128), F32)
    for h in range(2):
        rf[h, 0:rows, :] = zero
        rf[h, (n + 1) * rows:(n + 2) * rows, :] = zero

    def wait_x(k, carry):
        x_copy((me + k) % n, (me + k) % n).wait_recv()
        return carry

    lax.fori_loop(1, n, wait_x, 0)

    def widen(s, carry):
        for h in range(2):
            rf[h, pl.ds((s + 1) * rows, rows), :] = rx[s, :, h * 128:(h + 1) * 128].astype(F32)
        return carry

    lax.fori_loop(0, n, widen, 0)

    def spread(k, carry):
        r, v = k // vs, k % vs
        for b in range(3):
            for h in range(2):
                val = rf[h, pl.ds(b * rows + k, n, stride=rows), :].astype(BF16)
                xs[pl.ds((vs * b + v) * (rec * n) + r * n, n), h * 128:(h + 1) * 128] = val
        return carry

    lax.fori_loop(0, rows, spread, 0)

    def wait_w(k, carry):
        w_copy((me + k) % n, (me + k) % n).wait_recv()
        return carry

    lax.fori_loop(1, n, wait_w, 0)

    blank = jnp.zeros((gw, 128), BF16)
    for j in range(3):
        k2[(taps + 1 + j) * gw:(taps + 2 + j) * gw, 0:128] = blank
    for j in (0, 1, taps + 3):
        k2[j * gw:(j + 1) * gw, 128:256] = blank
    low = lax.broadcasted_iota(jnp.int32, (gw, 128), 1) < gw

    def put(j, val):
        k2[pl.ds(j * gw, gw), 0:128] = val
        k2[pl.ds((j + 2) * gw, gw), 128:256] = val

    def even(p):
        return jnp.where(low, ew[p + 1].astype(F32), ew[p].astype(F32)).astype(BF16)

    def build(p, carry):
        put(2 * p, even(p))
        e = ew[p + 1]
        put(2 * p + 1, jnp.concatenate([e[:, gw:], e[:, :gw]], axis=1))
        return carry

    lax.fori_loop(0, taps // 2, build, 0)
    put(taps, even(taps // 2))

    total_rows = vs * rec * n
    chunk = total_rows // 2

    def conv(c, carry):
        base = c * chunk
        acc = jnp.zeros((chunk, 256), F32)
        for q in range(taps // pack + 1):
            acc += mm(xs[pl.ds(base + q * rec * n, chunk), :], k2[q * 256:(q + 1) * 256, :])
        centre = xs[pl.ds(base + vs * rec * n, chunk), :].astype(F32)
        mixed = (centre + jax.nn.gelu(acc + bias_ref[...])).astype(BF16).astype(F32)
        for h in range(2):
            mf[h, pl.ds(base, chunk), :] = mixed[:, h * 128:(h + 1) * 128]
        return carry

    lax.fori_loop(0, 2, conv, 0)

    def gather(k, carry):
        for h in range(2):
            val = mf[h, pl.ds(k, vs, stride=rec * n), :].astype(BF16)
            m4[k // n, pl.ds((k % n) * vs, vs), h * 128:(h + 1) * 128] = val
        return carry

    lax.fori_loop(0, rec * n, gather, 0)

    def z_copy(r, slot):
        return pltpu.make_async_remote_copy(
            src_ref=m4.at[r], dst_ref=gg.at[slot],
            send_sem=z_send.at[r], recv_sem=g_recv.at[slot],
            device_id={"seq": r * per + own_h}, device_id_type=MESH,
        )

    for d in range(1, rec):
        z_copy((own_rec + d) % rec, me).start()
    gg[me] = m4[own_rec]
    core, line = own_h % 2, own_h // 2
    lines = per // 2
    sibling = own_rec * per + line * 2 + 1 - core

    def y_copy(d, slot, sem):
        return pltpu.make_async_remote_copy(
            src_ref=gg.at[slot], dst_ref=gg.at[slot],
            send_sem=y_send.at[sem], recv_sem=g_recv.at[slot],
            device_id={"seq": own_rec * per + ((line + d) % lines) * 2 + core}, device_id_type=MESH,
        )

    def c_copy(slot):
        return pltpu.make_async_remote_copy(
            src_ref=gg.at[slot], dst_ref=gg.at[slot],
            send_sem=c_send.at[slot], recv_sem=g_recv.at[slot],
            device_id={"seq": sibling}, device_id_type=MESH,
        )

    for e in range(rec):
        z = (own_rec + e) % rec
        slot = z * per + own_h
        if e:
            z_copy(z, slot).wait_recv()
        for d in range(1, lines):
            y_copy(d, slot, (d - 1) * rec + e).start()
        c_copy(slot).start()
    for e in range(rec):
        z = (own_rec + e) % rec
        for d in range(1, lines):
            slot = z * per + ((line + d) % lines) * 2 + core
            y_copy(d, slot, (d - 1) * rec + e).wait_recv()
            c_copy(slot).start()
    for e in range(rec):
        z = (own_rec + e) % rec
        for d in range(lines):
            slot = z * per + ((line + d) % lines) * 2 + 1 - core
            c_copy(slot).wait_recv()

    span = n * vs
    for gp in range(groups // 2):
        for ah in range(pack // 2):
            lo, hi = pair(
                gg[2 * gp, :, ah * 128:(ah + 1) * 128], gg[2 * gp + 1, :, ah * 128:(ah + 1) * 128]
            )
            block, lane = (gp * 128) // wide, (gp * 128) % wide
            lhs[block, 2 * ah, :, lane:lane + 128] = lo
            lhs[block, 2 * ah + 1, :, lane:lane + 128] = hi

    def r_copy(u, slot):
        return pltpu.make_async_remote_copy(
            src_ref=lhs.at[own_h, :, pl.ds(pl.multiple_of(u * vs, vs), vs)],
            dst_ref=res.at[slot % per, slot // per],
            send_sem=r_send.at[u], recv_sem=r_recv.at[slot],
            device_id={"seq": u}, device_id_type=MESH,
        )

    def start_r(k, carry):
        r_copy((me + k) % n, me).start()
        return carry

    lax.fori_loop(1, n, start_r, 0)
    res[own_h, own_rec] = lhs[own_h, :, pl.ds(pl.multiple_of(me * vs, vs), vs), :]

    def project(a, carry):
        total = mm(lhs[0, a], wq_ref[0:wide, :])
        for b in range(1, per):
            total += mm(lhs[b, a], wq_ref[b * wide:(b + 1) * wide, :])
        qkv[pl.ds(a * span, span), :] = total.astype(BF16)
        return carry

    lax.fori_loop(0, pack, project, 0)

    def t_copy(a, u, slot):
        return pltpu.make_async_remote_copy(
            src_ref=ct.at[a, pl.ds(pl.multiple_of(u * vs, vs), vs)],
            dst_ref=cx.at[slot % per, slot // per, a],
            send_sem=t_send.at[a, u], recv_sem=t_recv.at[a, slot],
            device_id={"seq": u}, device_id_type=MESH,
        )

    lane = lax.broadcasted_iota(jnp.int32, (span, wide), 1) // head

    def attend(a, carry):
        query = qkv[pl.ds(a * span, span), 0:wide].astype(F32) * (head ** -0.5)
        done = jnp.zeros((span, wide), F32)
        for h in range(wide // head):
            mine = jnp.where(lane == h, query, 0.0).astype(BF16)
            scores = lax.dot_general(
                mine, qkv[:, wide:2 * wide], (((1,), (1,)), ((), ())), preferred_element_type=F32
            )
            weights = jnp.exp(scores - jnp.max(scores, axis=1, keepdims=True))
            inverse = 1.0 / jnp.sum(weights, axis=1, keepdims=True)
            probs = (weights * inverse).astype(BF16)
            done = jnp.where(lane == h, mm(probs, qkv[:, 2 * wide:3 * wide]), done)
        ct[a] = done.astype(BF16)

        def start_t(k, c):
            t_copy(a, (me + k) % n, me).start()
            return c

        lax.fori_loop(1, n, start_t, 0)
        cx[own_h, own_rec, a] = ct[a, pl.ds(pl.multiple_of(me * vs, vs), vs), :]
        return carry

    lax.fori_loop(0, pack, attend, 0)

    def wait_t(k, carry):
        s = (me + k) % n
        r_copy(s, s).wait_recv()
        for a in range(pack):
            t_copy(a, s, s).wait_recv()
        return carry

    lax.fori_loop(1, n, wait_t, 0)

    total = mm(cx[0].reshape(count, wide), wo_ref[0:wide, :])
    for b in range(1, per):
        total += mm(cx[b].reshape(count, wide), wo_ref[b * wide:(b + 1) * wide, :])
    total += jnp.concatenate([res[b].reshape(count, wide).astype(F32) for b in range(per)], axis=1)
    mean = jnp.mean(total, axis=1, keepdims=True)
    centred = total - mean
    var = jnp.mean(centred * centred, axis=1, keepdims=True)
    normed = (centred / jnp.sqrt(var + 1e-05)).astype(BF16)
    r_o, t_o = ri // frames, ri % frames
    back = jnp.where(ci == r_o * frames + (t_o % pack) * vs + t_o // pack, 1.0, 0.0).astype(BF16)
    out_ref[...] = mm(back, normed).astype(BF16).reshape(rec, frames, width)

    def drain(k, carry):
        s = (me + k) % n
        x_copy(s, me).wait_send()
        w_copy(s, me).wait_send()
        r_copy(s, me).wait_send()
        for a in range(pack):
            t_copy(a, s, me).wait_send()
        return carry

    lax.fori_loop(1, n, drain, 0)
    for e in range(rec):
        z = (own_rec + e) % rec
        if e:
            z_copy(z, me).wait_send()
        for d in range(1, lines):
            y_copy(d, z * per + own_h, (d - 1) * rec + e).wait_send()
        for d in range(lines):
            c_copy(z * per + ((line + d) % lines) * 2 + core).wait_send()


def fused(n, frames, conv_weight, conv_bias, w_qkv, w_out):
    rec, frame_count, width = frames.shape
    heads, head = w_qkv.shape[2:]
    groups, taps = GROUPS, KERNEL
    gw = width // groups
    pack = 256 // gw
    vs = frame_count // pack
    rows = rec * vs
    per = n // rec
    wide = width // per
    tap_pairs = conv_weight.shape[0] // 2
    me = lax.axis_index("seq")
    mine = heads // per
    w_mine = lax.dynamic_slice_in_dim(w_qkv, (me % per) * mine, mine, 2).reshape(width, 3 * mine * head)
    bias = lax.dynamic_slice_in_dim(conv_bias, me * gw, gw)
    bias = jnp.tile(bias, pack).reshape(1, 256)
    vm = lambda *s: pltpu.VMEM(s, BF16)
    dma = lambda *s: pltpu.SemaphoreType.DMA(s)
    lines = per // 2
    return pl.pallas_call(
        functools.partial(fused_kernel, n, rec, groups, taps, head),
        out_shape=jax.ShapeDtypeStruct(frames.shape, BF16),
        in_specs=[pl.BlockSpec(memory_space=pltpu.VMEM)] * 5,
        out_specs=pl.BlockSpec(memory_space=pltpu.VMEM),
        scratch_shapes=[
            vm(n, rows, 256), vm(n, rows, 256), pltpu.VMEM((2, (n + 2) * rows, 128), F32),
            vm(3 * vs * rec * n, 256), vm(n, tap_pairs, gw, 128), vm(taps // 2 + 2, gw, 128),
            vm((taps + 4) * gw, 256), pltpu.VMEM((2, vs * rec * n, 128), F32),
            vm(rec, n * vs, 256), vm(n, n * vs, 256), vm(per, pack, n * vs, wide),
            vm(pack * n * vs, 3 * wide), vm(pack, n * vs, wide),
            vm(per, rec, pack, vs, wide), vm(per, rec, pack, vs, wide),
            dma(n), dma(n), dma(n), dma(n), dma(rec), dma(max(1, (lines - 1) * rec)), dma(n), dma(n),
            dma(n), dma(n), dma(pack, n), dma(pack, n),
        ],
        compiler_params=pltpu.CompilerParams(
            collective_id=0, has_side_effects=True, vmem_limit_bytes=56 * 2 ** 20
        ),
    )(frames, conv_weight, bias, w_mine, w_out.reshape(width, width))


def conv_part(source, kernel, groups):
    return lax.conv_general_dilated(
        source,
        kernel,
        (1,),
        "VALID",
        dimension_numbers=("NWC", "WIO", "NWC"),
        feature_group_count=groups,
        preferred_element_type=jnp.float32,
    )


def fits(n, frames, conv_weight, w_qkv):
    rec, frame_count, width = frames.shape
    heads, head = w_qkv.shape[2:]
    return (
        n == GROUPS
        and width == heads * head
        and width == GROUPS * 64
        and frame_count == KERNEL // 2
        and n % (2 * rec) == 0
        and heads % (n // rec) == 0
        and width * rec == 256 * n
    )


def body(frames, conv_weight, conv_bias, w_qkv, w_out):
    rec, frame_count, width = frames.shape
    devices = lax.axis_size("seq")
    if fits(devices, frames, conv_weight, w_qkv):
        return fused(devices, frames, conv_weight, conv_bias, w_qkv, w_out)
    group_width = width // GROUPS
    half = KERNEL // 2
    blocks = devices // GROUPS
    per_dev = rec // blocks
    tap_count = conv_weight.shape[0]
    spread = conv_weight.reshape(tap_count, group_width, 1, GROUPS, group_width)
    spread = jnp.broadcast_to(spread, (tap_count, group_width, blocks, GROUPS, group_width))
    spread = spread.reshape(tap_count, group_width, devices, group_width)
    kernel = lax.all_to_all(spread, "seq", split_axis=2, concat_axis=0, tiled=True).reshape(
        KERNEL, group_width, group_width
    )
    arranged = frames.reshape(blocks, per_dev, frame_count, GROUPS, group_width)
    arranged = jnp.transpose(arranged, (0, 3, 1, 2, 4)).reshape(
        devices, per_dev, frame_count, group_width
    )
    length = frame_count * devices
    inputs = lax.all_to_all(arranged, "seq", split_axis=0, concat_axis=2, tiled=True).reshape(
        per_dev, length, group_width
    )
    padded = jnp.pad(inputs, ((0, 0), (half, half - 1), (0, 0)))
    conv = conv_part(padded, kernel, 1)
    group_index = lax.axis_index("seq") % GROUPS
    bias = lax.dynamic_slice_in_dim(conv_bias, group_index * group_width, group_width)
    local = (inputs.astype(jnp.float32) + jax.nn.gelu(conv + bias)).astype(jnp.bfloat16)
    sending = local.reshape(1, per_dev, devices, frame_count, group_width)
    returned = lax.all_to_all(sending, "seq", split_axis=2, concat_axis=0, tiled=True)
    returned = returned.reshape(blocks, GROUPS, per_dev, frame_count, group_width)
    mixed = jnp.transpose(returned, (0, 2, 3, 1, 4)).reshape(rec, frame_count, width)
    heads = w_qkv.shape[2]
    head = w_qkv.shape[3]
    items = rec * heads // devices
    projected = jnp.einsum(
        "btd,dshe->bhtse", mixed, w_qkv, preferred_element_type=jnp.float32
    ).astype(jnp.bfloat16)
    packed = projected.reshape(devices, items, frame_count, 3 * head)
    scale = head ** (-0.5)
    portion = lax.all_to_all(packed, "seq", split_axis=0, concat_axis=2, tiled=True)
    count = portion.shape[1]
    length = portion.shape[2]
    grid = portion.reshape(count, length, 3, head)
    block = math.gcd(length, 512)

    def one(item):
        query = item[:, 0]
        keys = item[:, 1]
        values = item[:, 2]

        def rows(query_block):
            scores = (
                jnp.einsum("qe,ke->qk", query_block, keys, preferred_element_type=jnp.float32)
                * scale
            )
            top = jnp.max(scores, axis=1, keepdims=True)
            weights = jnp.exp(scores - top)
            probs = (weights / jnp.sum(weights, axis=1, keepdims=True)).astype(jnp.bfloat16)
            return jnp.dot(probs, values, preferred_element_type=jnp.float32).astype(jnp.bfloat16)

        return lax.map(rows, query.reshape(length // block, block, head)).reshape(length, head)

    attended = lax.map(one, grid)
    context = lax.all_to_all(attended[None], "seq", split_axis=2, concat_axis=0, tiled=True)
    context = context.reshape(rec, heads, frame_count, head)
    out = jnp.einsum("bhte,hed->btd", context, w_out, preferred_element_type=jnp.float32)
    total = mixed.astype(jnp.float32) + out
    mean = jnp.mean(total, axis=2, keepdims=True)
    centered = total - mean
    var = jnp.mean(centered * centered, axis=2, keepdims=True)
    return (centered / jnp.sqrt(var + 1e-05)).astype(jnp.bfloat16)


def solution(mesh):
    return jax.shard_map(
        body,
        mesh=mesh,
        in_specs=(P("parts", "seq", None), P("seq", None, None), P(), P(), P()),
        out_specs=P("parts", "seq", None),
        check_vma=False,
    )
```

profile of v0, /device:TPU:0, one launch (start us, length us, event | category | flops | bytes accessed | tf_op | source)
XLA Modules:
  0.0 111.3 jit_solution(3440564672154239995)
XLA Ops:
  0.0 1.6 %constant_dynamic-slice_fusion = bf16[1024,3,4,64]{0,3,2,1:T(8,128)(2,1)S(1)} fusion(bf16[1024,3,16,64]{0,3,2,1:T(8,128)(2,1)} %param.8, s32[]{:T(128)S(6)} %select_n.15), kind=kLoop, calls=%fused_computation | loop fusion | bytes 3145732 | tf_op jit(solution)/shard_map/dynamic_slice | solution.py:366
  1.6 1.6 %copy.7.wq_ref = bf16[1024,768]{1,0:T(8,128)(2,1)} copy(bf16[1024,768]{0,1:T(8,128)(2,1)S(1)} %bitcast.2) | data formatting | bytes 3145728 | tf_op jit(solution)/shard_map/reshape | solution.py:366
  3.2 0.8 dynamic_slice.6
  4.0 0.6 reshape_tile.3.bias_ref
  4.6 104.8 %shard_map.55 = bf16[4,64,1024]{2,1,0:T(8,128)(2,1)} custom-call(bf16[4,64,1024]{2,1,0:T(8,128)(2,1)} %x_ref.1, bf16[8,64,1024]{2,1,0:T(8,128)(2,1)} %w_ref.1, f32[1,256]{1,0:T(1,128)} %reshape_tile.3.bias_ref, bf16[1024,768]{1,0:T(8,128)(2,1)} %copy.7.wq_ref, bf16[1024,1024]{1,0:T(8,128)(2,1)} %bitcast.3), custom_call_target="tpu_custom_call" | custom-call | tf_op jit(solution)/shard_map/pallas_call | solution.py:372
  109.4 1.9 %copy.9 = bf16[4,64,1024]{2,1,0:T(8,128)(2,1)} copy(bf16[4,64,1024]{2,1,0:T(8,128)(2,1)} %shard_map.55) | data formatting | bytes 1048576
  (1 shorter events, 0.0 us)
where the time goes:
time: 112 us; the launch traced here: 111 us
  Pallas kernels  105 us (94%)
  local copies, waits for them, and re-layouts  6.48 us (6%)
    pallas_call x1, Pallas kernels, fused(): pl.pallas_call(functools.partial(fused_kernel, n, rec, groups, taps, head...  105 us

commit v1 on v0

--- a/solution.py
+++ b/solution.py
@@ -28,11 +28,11 @@
 
 
 def fused_kernel(
-    n, rec, groups, taps, head,
-    x_ref, w_ref, bias_ref, wq_ref, wo_ref, out_ref,
-    sx, rx, rf, xs, sw, ew, k2, mf, m4, gg, lhs, qkv, ct, cx, res,
-    sx_send, sx_recv, sw_send, sw_recv, z_send, y_send, c_send, g_recv,
-    r_send, r_recv, t_send, t_recv,
+    n, parts, rec, groups, taps, head,
+    x_ref, w_ref, bias_ref, wq_hbm, wo_hbm, out_ref,
+    sx, rx, rf, xs, sw, ew, k2, mf, m4, gg, lhs, qacc, qkv, ct, cx, res, wq_ref, wo_ref,
+    sx_send, sx_recv, sw_send, sw_recv, f_send, f_recv, z_send, y_send, c_send, g_recv,
+    r_send, r_recv, t_send, t_recv, l_sem,
 ):
     me = lax.axis_index("seq")
     width = x_ref.shape[2]
@@ -44,6 +44,8 @@
     per = n // rec
     wide = width // per
     tap_pairs = w_ref.shape[0] // 2
+    share = tap_pairs // parts
+    part = lax.axis_index("parts") if parts > 1 else 0
     own_rec = me // per
     own_h = me % per
 
@@ -54,6 +56,65 @@
         return carry
 
     lax.fori_loop(1, n, greet, 0)
+    for d in range(1, parts):
+        pl.semaphore_signal(
+            barrier, inc=1, device_id={"parts": (part + d) % parts, "seq": me}, device_id_type=MESH
+        )
+    wq_load = pltpu.make_async_copy(wq_hbm, wq_ref, l_sem.at[0])
+    wo_load = pltpu.make_async_copy(wo_hbm, wo_ref, l_sem.at[1])
+
+    def x_copy(peer, slot):
+        return pltpu.make_async_remote_copy(
+            src_ref=sx.at[peer], dst_ref=rx.at[slot],
+            send_sem=sx_send.at[peer], recv_sem=sx_recv.at[slot],
+            device_id={"seq": peer}, device_id_type=MESH,
+        )
+
+    def w_copy(peer, slot):
+        return pltpu.make_async_remote_copy(
+            src_ref=sw.at[peer], dst_ref=ew.at[pl.ds(1 + slot * tap_pairs + part * share, share)],
+            send_sem=sw_send.at[peer], recv_sem=sw_recv.at[slot],
+            device_id={"seq": peer}, device_id_type=MESH,
+        )
+
+    for p in range(share):
+        for gp in range(groups // 2):
+            tap = 2 * (part * share + p)
+            lo, hi = pair(
+                w_ref[tap, :, gp * 128:(gp + 1) * 128], w_ref[tap + 1, :, gp * 128:(gp + 1) * 128]
+            )
+            sw[2 * gp, p] = lo
+            sw[2 * gp + 1, p] = hi
+
+    pl.semaphore_wait(barrier, n - 1 + parts - 1)
+
+    def start_w(k, carry):
+        w_copy((me + k) % n, me).start()
+        return carry
+
+    lax.fori_loop(1, n, start_w, 0)
+
+    ew[pl.ds(1 + me * tap_pairs + part * share, share)] = sw[me]
+
+    def f_copy(d, slot):
+        return pltpu.make_async_remote_copy(
+            src_ref=ew.at[pl.ds(1 + slot * tap_pairs + part * share, share)],
+            dst_ref=ew.at[pl.ds(1 + slot * tap_pairs + part * share, share)],
+            send_sem=f_send.at[d - 1, slot], recv_sem=f_recv.at[d - 1, slot],
+            device_id={"parts": (part + d) % parts, "seq": me}, device_id_type=MESH,
+        )
+
+    def f_wait(d, slot):
+        source = (part + parts - d) % parts
+        return pltpu.make_async_remote_copy(
+            src_ref=ew.at[pl.ds(1 + slot * tap_pairs + source * share, share)],
+            dst_ref=ew.at[pl.ds(1 + slot * tap_pairs + source * share, share)],
+            send_sem=f_send.at[d - 1, slot], recv_sem=f_recv.at[d - 1, slot],
+            device_id={"parts": (part + d) % parts, "seq": me}, device_id_type=MESH,
+        )
+
+    for d in range(1, parts):
+        f_copy(d, me).start()
 
     count = rec * frames
     ri = lax.broadcasted_iota(jnp.int32, (count, count), 0)
@@ -72,44 +133,14 @@
             sx[2 * gp, :, ah * 128:(ah + 1) * 128] = lo
             sx[2 * gp + 1, :, ah * 128:(ah + 1) * 128] = hi
 
-    pl.semaphore_wait(barrier, n - 1)
-
-    def x_copy(peer, slot):
-        return pltpu.make_async_remote_copy(
-            src_ref=sx.at[peer], dst_ref=rx.at[slot],
-            send_sem=sx_send.at[peer], recv_sem=sx_recv.at[slot],
-            device_id={"seq": peer}, device_id_type=MESH,
-        )
-
-    def w_copy(peer, slot):
-        return pltpu.make_async_remote_copy(
-            src_ref=sw.at[peer], dst_ref=ew.at[pl.ds(1 + slot * tap_pairs, tap_pairs)],
-            send_sem=sw_send.at[peer], recv_sem=sw_recv.at[slot],
-            device_id={"seq": peer}, device_id_type=MESH,
-        )
-
     def start_x(k, carry):
         x_copy((me + k) % n, me).start()
         return carry
 
     lax.fori_loop(1, n, start_x, 0)
-    for p in range(tap_pairs):
-        for gp in range(groups // 2):
-            lo, hi = pair(
-                w_ref[2 * p, :, gp * 128:(gp + 1) * 128],
-                w_ref[2 * p + 1, :, gp * 128:(gp + 1) * 128],
-            )
-            sw[2 * gp, p] = lo
-            sw[2 * gp + 1, p] = hi
-
-    def start_w(k, carry):
-        w_copy((me + k) % n, me).start()
-        return carry
-
-    lax.fori_loop(1, n, start_w, 0)
-
+    wq_load.start()
+    wo_load.start()
     rx[me] = sx[me]
-    ew[pl.ds(1 + me * tap_pairs, tap_pairs)] = sw[me]
     ew[0] = jnp.zeros_like(ew[0])
     ew[taps // 2 + 1] = jnp.zeros_like(ew[0])
     zero = jnp.zeros((rows, 128), F32)
@@ -117,34 +148,21 @@
         rf[h, 0:rows, :] = zero
         rf[h, (n + 1) * rows:(n + 2) * rows, :] = zero
 
-    def wait_x(k, carry):
-        x_copy((me + k) % n, (me + k) % n).wait_recv()
-        return carry
-
-    lax.fori_loop(1, n, wait_x, 0)
-
-    def widen(s, carry):
-        for h in range(2):
-            rf[h, pl.ds((s + 1) * rows, rows), :] = rx[s, :, h * 128:(h + 1) * 128].astype(F32)
-        return carry
-
-    lax.fori_loop(0, n, widen, 0)
-
-    def spread(k, carry):
-        r, v = k // vs, k % vs
-        for b in range(3):
-            for h in range(2):
-                val = rf[h, pl.ds(b * rows + k, n, stride=rows), :].astype(BF16)
-                xs[pl.ds((vs * b + v) * (rec * n) + r * n, n), h * 128:(h + 1) * 128] = val
-        return carry
-
-    lax.fori_loop(0, rows, spread, 0)
-
     def wait_w(k, carry):
-        w_copy((me + k) % n, (me + k) % n).wait_recv()
+        s = (me + n - k) % n
+        w_copy(s, s).wait_recv()
+        for d in range(1, parts):
+            f_copy(d, s).start()
         return carry
 
     lax.fori_loop(1, n, wait_w, 0)
+
+    def wait_f(k, carry):
+        for d in range(1, parts):
+            f_wait(d, (me + n - k) % n).wait_recv()
+        return carry
+
+    lax.fori_loop(0, n, wait_f, 0)
 
     blank = jnp.zeros((gw, 128), BF16)
     for j in range(3):
@@ -169,29 +187,35 @@
     lax.fori_loop(0, taps // 2, build, 0)
     put(taps, even(taps // 2))
 
-    total_rows = vs * rec * n
-    chunk = total_rows // 2
-
-    def conv(c, carry):
-        base = c * chunk
-        acc = jnp.zeros((chunk, 256), F32)
-        for q in range(taps // pack + 1):
-            acc += mm(xs[pl.ds(base + q * rec * n, chunk), :], k2[q * 256:(q + 1) * 256, :])
-        centre = xs[pl.ds(base + vs * rec * n, chunk), :].astype(F32)
-        mixed = (centre + jax.nn.gelu(acc + bias_ref[...])).astype(BF16).astype(F32)
+    def widen(k, carry):
+        s = (me + n - k) % n
+
+        @pl.when(k > 0)
+        def _():
+            x_copy(s, s).wait_recv()
+
         for h in range(2):
-            mf[h, pl.ds(base, chunk), :] = mixed[:, h * 128:(h + 1) * 128]
-        return carry
-
-    lax.fori_loop(0, 2, conv, 0)
-
-    def gather(k, carry):
-        for h in range(2):
-            val = mf[h, pl.ds(k, vs, stride=rec * n), :].astype(BF16)
-            m4[k // n, pl.ds((k % n) * vs, vs), h * 128:(h + 1) * 128] = val
-        return carry
-
-    lax.fori_loop(0, rec * n, gather, 0)
+            rf[h, pl.ds((s + 1) * rows, rows), :] = rx[s, :, h * 128:(h + 1) * 128].astype(F32)
+        return carry
+
+    lax.fori_loop(0, n, widen, 0)
+
+    def spread(k, carry):
+        r, v = k // vs, k % vs
+        for b in range(3):
+            for h in range(2):
+                val = rf[h, pl.ds(b * rows + k, n, stride=rows), :].astype(BF16)
+                xs[vs * b + v, r, :, h * 128:(h + 1) * 128] = val
+        return carry
+
+    lax.fori_loop(0, rows, spread, 0)
+
+    pairs = rec // 2
+    chunk = vs * 2 * n
+    w2 = bias_ref[:, pl.ds(pl.multiple_of((me // 2) * 128, 128), 128)]
+    lo, hi = pair(w2, w2)
+    bias = jnp.where(me % 2 == 0, lo, hi)
+    bias = jnp.concatenate([bias, bias], axis=1)
 
     def z_copy(r, slot):
         return pltpu.make_async_remote_copy(
@@ -200,8 +224,28 @@
             device_id={"seq": r * per + own_h}, device_id_type=MESH,
         )
 
-    for d in range(1, rec):
-        z_copy((own_rec + d) % rec, me).start()
+    for i in range(pairs):
+        cp = (own_rec // 2 + 1 + i) % pairs
+        acc = jnp.zeros((chunk, 256), F32)
+        for q in range(taps // pack + 1):
+            acc += mm(
+                xs[q:q + vs, pl.ds(2 * cp, 2)].reshape(chunk, 256), k2[q * 256:(q + 1) * 256, :]
+            )
+        centre = xs[vs:2 * vs, pl.ds(2 * cp, 2)].reshape(chunk, 256).astype(F32)
+        mixed = (centre + jax.nn.gelu(acc + bias)).astype(BF16).astype(F32)
+        for h in range(2):
+            mf[h] = mixed[:, h * 128:(h + 1) * 128]
+
+        def gather(k, carry):
+            for h in range(2):
+                val = mf[h, pl.ds(k, vs, stride=2 * n), :].astype(BF16)
+                m4[2 * cp + k // n, pl.ds((k % n) * vs, vs), h * 128:(h + 1) * 128] = val
+            return carry
+
+        lax.fori_loop(0, 2 * n, gather, 0)
+        for j in range(2):
+            if i < pairs - 1 or j:
+                z_copy(2 * cp + (own_rec + j) % 2, me).start()
     gg[me] = m4[own_rec]
     core, line = own_h % 2, own_h // 2
     lines = per // 2
@@ -221,35 +265,65 @@
             device_id={"seq": sibling}, device_id_type=MESH,
         )
 
-    for e in range(rec):
-        z = (own_rec + e) % rec
+    wq_load.wait()
+    wo_load.wait()
+    span = n * vs
+
+    def step_a(e, z):
         slot = z * per + own_h
         if e:
             z_copy(z, slot).wait_recv()
         for d in range(1, lines):
             y_copy(d, slot, (d - 1) * rec + e).start()
         c_copy(slot).start()
-    for e in range(rec):
-        z = (own_rec + e) % rec
+
+    def step_b(e, z):
         for d in range(1, lines):
             slot = z * per + ((line + d) % lines) * 2 + core
             y_copy(d, slot, (d - 1) * rec + e).wait_recv()
             c_copy(slot).start()
-    for e in range(rec):
-        z = (own_rec + e) % rec
+
+    def step_c(e, z):
         for d in range(lines):
-            slot = z * per + ((line + d) % lines) * 2 + 1 - core
-            c_copy(slot).wait_recv()
-
-    span = n * vs
-    for gp in range(groups // 2):
-        for ah in range(pack // 2):
-            lo, hi = pair(
-                gg[2 * gp, :, ah * 128:(ah + 1) * 128], gg[2 * gp + 1, :, ah * 128:(ah + 1) * 128]
-            )
-            block, lane = (gp * 128) // wide, (gp * 128) % wide
-            lhs[block, 2 * ah, :, lane:lane + 128] = lo
-            lhs[block, 2 * ah + 1, :, lane:lane + 128] = hi
+            c_copy(z * per + ((line + d) % lines) * 2 + 1 - core).wait_recv()
+        for gl in range(per // 2):
+            for ah in range(pack // 2):
+                g = z * per + 2 * gl
+                lo, hi = pair(
+                    gg[g, :, ah * 128:(ah + 1) * 128], gg[g + 1, :, ah * 128:(ah + 1) * 128]
+                )
+                lhs[z, 2 * ah, :, gl * 128:(gl + 1) * 128] = lo
+                lhs[z, 2 * ah + 1, :, gl * 128:(gl + 1) * 128] = hi
+
+        def project(a, carry):
+            at = pl.ds(a * span, span)
+            total = mm(lhs[z, a], wq_ref[pl.ds(pl.multiple_of(z * wide, wide), wide), :])
+            if e:
+                total += qacc[at, :]
+            if e == rec - 1:
+                qkv[at, :] = total.astype(BF16)
+            else:
+                qacc[at, :] = total
+            return carry
+
+        lax.fori_loop(0, pack, project, 0)
+
+    mate = (own_rec // 2) * 2 + 1 - own_rec % 2
+    others = [
+        2 * ((own_rec // 2 + 1 + i) % pairs) + (own_rec + j) % 2
+        for i in range(pairs - 1) for j in range(2)
+    ]
+    zs = list(enumerate([own_rec] + others + [mate]))
+    for e, z in zs[:-1]:
+        step_a(e, z)
+    for e, z in zs[:-1]:
+        step_b(e, z)
+    step_a(*zs[-1])
+    for e, z in zs[:-2]:
+        step_c(e, z)
+    step_b(*zs[-1])
+    for e, z in zs[-2:]:
+        step_c(e, z)
 
     def r_copy(u, slot):
         return pltpu.make_async_remote_copy(
@@ -265,15 +339,6 @@
 
     lax.fori_loop(1, n, start_r, 0)
     res[own_h, own_rec] = lhs[own_h, :, pl.ds(pl.multiple_of(me * vs, vs), vs), :]
-
-    def project(a, carry):
-        total = mm(lhs[0, a], wq_ref[0:wide, :])
-        for b in range(1, per):
-            total += mm(lhs[b, a], wq_ref[b * wide:(b + 1) * wide, :])
-        qkv[pl.ds(a * span, span), :] = total.astype(BF16)
-        return carry
-
-    lax.fori_loop(0, pack, project, 0)
 
     def t_copy(a, u, slot):
         return pltpu.make_async_remote_copy(
@@ -340,8 +405,10 @@
         return carry
 
     lax.fori_loop(1, n, drain, 0)
-    for e in range(rec):
-        z = (own_rec + e) % rec
+    for d in range(1, parts):
+        for s in range(n):
+            f_copy(d, s).wait_send()
+    for e, z in zs:
         if e:
             z_copy(z, me).wait_send()
         for d in range(1, lines):
@@ -364,25 +431,29 @@
     me = lax.axis_index("seq")
     mine = heads // per
     w_mine = lax.dynamic_slice_in_dim(w_qkv, (me % per) * mine, mine, 2).reshape(width, 3 * mine * head)
-    bias = lax.dynamic_slice_in_dim(conv_bias, me * gw, gw)
-    bias = jnp.tile(bias, pack).reshape(1, 256)
+    bias = conv_bias.reshape(1, width)
+    parts = lax.axis_size("parts")
+    if tap_pairs % parts:
+        parts = 1
     vm = lambda *s: pltpu.VMEM(s, BF16)
     dma = lambda *s: pltpu.SemaphoreType.DMA(s)
     lines = per // 2
     return pl.pallas_call(
-        functools.partial(fused_kernel, n, rec, groups, taps, head),
+        functools.partial(fused_kernel, n, parts, rec, groups, taps, head),
         out_shape=jax.ShapeDtypeStruct(frames.shape, BF16),
-        in_specs=[pl.BlockSpec(memory_space=pltpu.VMEM)] * 5,
+        in_specs=[pl.BlockSpec(memory_space=pltpu.VMEM)] * 3 + [pl.BlockSpec(memory_space=pl.ANY)] * 2,
         out_specs=pl.BlockSpec(memory_space=pltpu.VMEM),
         scratch_shapes=[
             vm(n, rows, 256), vm(n, rows, 256), pltpu.VMEM((2, (n + 2) * rows, 128), F32),
-            vm(3 * vs * rec * n, 256), vm(n, tap_pairs, gw, 128), vm(taps // 2 + 2, gw, 128),
-            vm((taps + 4) * gw, 256), pltpu.VMEM((2, vs * rec * n, 128), F32),
+            vm(3 * vs, rec, n, 256), vm(n, tap_pairs // parts, gw, 128), vm(taps // 2 + 2, gw, 128),
+            vm((taps + 4) * gw, 256), pltpu.VMEM((2, vs * 2 * n, 128), F32),
             vm(rec, n * vs, 256), vm(n, n * vs, 256), vm(per, pack, n * vs, wide),
-            vm(pack * n * vs, 3 * wide), vm(pack, n * vs, wide),
+            pltpu.VMEM((pack * n * vs, 3 * wide), F32), vm(pack * n * vs, 3 * wide), vm(pack, n * vs, wide),
             vm(per, rec, pack, vs, wide), vm(per, rec, pack, vs, wide),
-            dma(n), dma(n), dma(n), dma(n), dma(rec), dma(max(1, (lines - 1) * rec)), dma(n), dma(n),
-            dma(n), dma(n), dma(pack, n), dma(pack, n),
+            vm(width, 3 * wide), vm(width, width),
+            dma(n), dma(n), dma(n), dma(n),
+            dma(max(1, parts - 1), n), dma(max(1, parts - 1), n), dma(rec), dma(max(1, (lines - 1) * rec)), dma(n), dma(n),
+            dma(n), dma(n), dma(pack, n), dma(pack, n), dma(2),
         ],
         compiler_params=pltpu.CompilerParams(
             collective_id=0, has_side_effects=True, vmem_limit_bytes=56 * 2 ** 20
@@ -411,6 +482,9 @@
         and width == GROUPS * 64
         and frame_count == KERNEL // 2
         and n % (2 * rec) == 0
+        and rec % 2 == 0
+        and n * 64 == 256 * rec
+        and conv_weight.shape[0] % 2 == 0
         and heads % (n // rec) == 0
         and width * rec == 256 * n
     )

time: 112 us -> 99.8 us (0.89)
  Pallas kernels: 105 us -> 94.5 us
  local copies, waits for them, and re-layouts: 6.48 us -> 5.07 us
    pallas_call x1, Pallas kernels: 105 us -> 94.5 us  [fused(): pl.pallas_call(functools.partial(fused_kernel, n, parts, rec, groups, tap...]
where the time goes in v1:
time: 99.8 us; the launch traced here: 99.6 us
  Pallas kernels  94.5 us (95%)
  local copies, waits for them, and re-layouts  5.07 us (5%)
    pallas_call x1, Pallas kernels, fused(): pl.pallas_call(functools.partial(fused_kernel, n, parts, rec, groups, tap...  94.5 us

profile of v1, /device:TPU:0, one launch (start us, length us, event | category | flops | bytes accessed | tf_op | source)
XLA Modules:
  0.0 99.6 jit_solution(182525029276557434)
XLA Ops:
  0.0 1.6 %constant_dynamic-slice_fusion = bf16[1024,3,4,64]{0,3,2,1:T(8,128)(2,1)S(1)} fusion(bf16[1024,3,16,64]{0,3,2,1:T(8,128)(2,1)} %param.8, s32[]{:T(128)S(6)} %select_n.11), kind=kLoop, calls=%fused_computation | loop fusion | bytes 3145732 | tf_op jit(solution)/shard_map/dynamic_slice | solution.py:433
  1.6 1.6 %copy.7.wq_hbm = bf16[1024,768]{1,0:T(8,128)(2,1)} copy(bf16[1024,768]{0,1:T(8,128)(2,1)S(1)} %bitcast.3) | data formatting | bytes 3145728 | tf_op jit(solution)/shard_map/reshape | solution.py:433
  3.2 94.5 %shard_map.55 = bf16[4,64,1024]{2,1,0:T(8,128)(2,1)} custom-call(bf16[4,64,1024]{2,1,0:T(8,128)(2,1)} %x_ref.1, bf16[8,64,1024]{2,1,0:T(8,128)(2,1)} %w_ref.1, f32[1,1024]{1,0:T(1,128)} %bitcast.5, bf16[1024,768]{1,0:T(8,128)(2,1)} %copy.7.wq_hbm, bf16[1024,1024]{1,0:T(8,128)(2,1)} %bitcast.4), custom_call_target="tpu_custom_call" | custom-call | tf_op jit(solution)/shard_map/pallas_call | solution.py:441
  97.7 1.9 %copy.9 = bf16[4,64,1024]{2,1,0:T(8,128)(2,1)} copy(bf16[4,64,1024]{2,1,0:T(8,128)(2,1)} %shard_map.55) | data formatting | bytes 1048576

commit v2 on v1

--- a/solution.py
+++ b/solution.py
@@ -30,7 +30,7 @@
 def fused_kernel(
     n, parts, rec, groups, taps, head,
     x_ref, w_ref, bias_ref, wq_hbm, wo_hbm, out_ref,
-    sx, rx, rf, xs, sw, ew, k2, mf, m4, gg, lhs, qacc, qkv, ct, cx, res, wq_ref, wo_ref,
+    sx, rx, rf, xs, sw, ew, k2, mf, m4, gg, lhs, qacc, qkv, ct, cx, res, rs, wq_ref, wo_ref,
     sx_send, sx_recv, sw_send, sw_recv, f_send, f_recv, z_send, y_send, c_send, g_recv,
     r_send, r_recv, t_send, t_recv, l_sem,
 ):
@@ -247,6 +247,21 @@
             if i < pairs - 1 or j:
                 z_copy(2 * cp + (own_rec + j) % 2, me).start()
     gg[me] = m4[own_rec]
+
+    def r_copy(u, slot):
+        return pltpu.make_async_remote_copy(
+            src_ref=m4.at[:, pl.ds(pl.multiple_of(u * vs, vs), vs)],
+            dst_ref=res.at[slot],
+            send_sem=r_send.at[u], recv_sem=r_recv.at[slot],
+            device_id={"seq": u}, device_id_type=MESH,
+        )
+
+    def start_r(k, carry):
+        r_copy((me + k) % n, me).start()
+        return carry
+
+    lax.fori_loop(1, n, start_r, 0)
+    res[me] = m4[:, pl.ds(pl.multiple_of(me * vs, vs), vs), :]
     core, line = own_h % 2, own_h // 2
     lines = per // 2
     sibling = own_rec * per + line * 2 + 1 - core
@@ -325,21 +340,6 @@
     for e, z in zs[-2:]:
         step_c(e, z)
 
-    def r_copy(u, slot):
-        return pltpu.make_async_remote_copy(
-            src_ref=lhs.at[own_h, :, pl.ds(pl.multiple_of(u * vs, vs), vs)],
-            dst_ref=res.at[slot % per, slot // per],
-            send_sem=r_send.at[u], recv_sem=r_recv.at[slot],
-            device_id={"seq": u}, device_id_type=MESH,
-        )
-
-    def start_r(k, carry):
-        r_copy((me + k) % n, me).start()
-        return carry
-
-    lax.fori_loop(1, n, start_r, 0)
-    res[own_h, own_rec] = lhs[own_h, :, pl.ds(pl.multiple_of(me * vs, vs), vs), :]
-
     def t_copy(a, u, slot):
         return pltpu.make_async_remote_copy(
             src_ref=ct.at[a, pl.ds(pl.multiple_of(u * vs, vs), vs)],
@@ -374,9 +374,23 @@
 
     lax.fori_loop(0, pack, attend, 0)
 
+    def wait_r(k, carry):
+        s = (me + n - k) % n
+        r_copy(s, s).wait_recv()
+        return carry
+
+    lax.fori_loop(1, n, wait_r, 0)
+    for gp in range(groups // 2):
+        for ah in range(pack // 2):
+            lo, hi = pair(
+                res[2 * gp, :, :, ah * 128:(ah + 1) * 128].reshape(rows, 128),
+                res[2 * gp + 1, :, :, ah * 128:(ah + 1) * 128].reshape(rows, 128),
+            )
+            rs[:, 2 * ah, :, gp * 128:(gp + 1) * 128] = lo.reshape(rec, vs, 128)
+            rs[:, 2 * ah + 1, :, gp * 128:(gp + 1) * 128] = hi.reshape(rec, vs, 128)
+
     def wait_t(k, carry):
-        s = (me + k) % n
-        r_copy(s, s).wait_recv()
+        s = (me + n - k) % n
         for a in range(pack):
             t_copy(a, s, s).wait_recv()
         return carry
@@ -386,7 +400,7 @@
     total = mm(cx[0].reshape(count, wide), wo_ref[0:wide, :])
     for b in range(1, per):
         total += mm(cx[b].reshape(count, wide), wo_ref[b * wide:(b + 1) * wide, :])
-    total += jnp.concatenate([res[b].reshape(count, wide).astype(F32) for b in range(per)], axis=1)
+    total += rs[...].reshape(count, width).astype(F32)
     mean = jnp.mean(total, axis=1, keepdims=True)
     centred = total - mean
     var = jnp.mean(centred * centred, axis=1, keepdims=True)
@@ -449,7 +463,7 @@
             vm((taps + 4) * gw, 256), pltpu.VMEM((2, vs * 2 * n, 128), F32),
             vm(rec, n * vs, 256), vm(n, n * vs, 256), vm(per, pack, n * vs, wide),
             pltpu.VMEM((pack * n * vs, 3 * wide), F32), vm(pack * n * vs, 3 * wide), vm(pack, n * vs, wide),
-            vm(per, rec, pack, vs, wide), vm(per, rec, pack, vs, wide),
+            vm(per, rec, pack, vs, wide), vm(n, rec, vs, 256), vm(rec, pack, vs, width),
             vm(width, 3 * wide), vm(width, width),
             dma(n), dma(n), dma(n), dma(n),
             dma(max(1, parts - 1), n), dma(max(1, parts - 1), n), dma(rec), dma(max(1, (lines - 1) * rec)), dma(n), dma(n),

time: 99.8 us -> 96.3 us (0.965)
  Pallas kernels: 94.5 us -> 91 us
    pallas_call x1, Pallas kernels: 94.5 us -> 91 us  [fused(): pl.pallas_call(functools.partial(fused_kernel, n, parts, rec, groups, tap...]
where the time goes in v2:
time: 96.3 us; the launch traced here: 96.1 us
  Pallas kernels  91 us (94%)
  local copies, waits for them, and re-layouts  5.07 us (5%)
    pallas_call x1, Pallas kernels, fused(): pl.pallas_call(functools.partial(fused_kernel, n, parts, rec, groups, tap...  91 us

profile of v2, /device:TPU:0, one launch (start us, length us, event | category | flops | bytes accessed | tf_op | source)
XLA Modules:
  0.0 96.1 jit_solution(266926300865202140)
XLA Ops:
  0.0 1.6 %constant_dynamic-slice_fusion = bf16[1024,3,4,64]{0,3,2,1:T(8,128)(2,1)S(1)} fusion(bf16[1024,3,16,64]{0,3,2,1:T(8,128)(2,1)} %param.8, s32[]{:T(128)S(6)} %select_n.11), kind=kLoop, calls=%fused_computation | loop fusion | bytes 3145732 | tf_op jit(solution)/shard_map/dynamic_slice | solution.py:447
  1.6 1.6 %copy.7.wq_hbm = bf16[1024,768]{1,0:T(8,128)(2,1)} copy(bf16[1024,768]{0,1:T(8,128)(2,1)S(1)} %bitcast.3) | data formatting | bytes 3145728 | tf_op jit(solution)/shard_map/reshape | solution.py:447
  3.2 91.0 %shard_map.55 = bf16[4,64,1024]{2,1,0:T(8,128)(2,1)} custom-call(bf16[4,64,1024]{2,1,0:T(8,128)(2,1)} %x_ref.1, bf16[8,64,1024]{2,1,0:T(8,128)(2,1)} %w_ref.1, f32[1,1024]{1,0:T(1,128)} %bitcast.5, bf16[1024,768]{1,0:T(8,128)(2,1)} %copy.7.wq_hbm, bf16[1024,1024]{1,0:T(8,128)(2,1)} %bitcast.4), custom_call_target="tpu_custom_call" | custom-call | tf_op jit(solution)/shard_map/pallas_call | solution.py:455
  94.3 1.9 %copy.9 = bf16[4,64,1024]{2,1,0:T(8,128)(2,1)} copy(bf16[4,64,1024]{2,1,0:T(8,128)(2,1)} %shard_map.55) | data formatting | bytes 1048576
